TPU v7x, 512 devices: a whole 4x8x8 slice. The times are simulated.
512 devices in a mesh: grp: 32 (over y, x), mlp: 16 (over z, core).
Axes of the slice: x: 4, y: 8, z: 8, core: 2. Of those that a mesh axis runs over, the one named last changes fastest.
Arguments:
- queries: bfloat16 [32, 128, 4096], P('grp'), may hold values from -70 to 70
- fresh_kv: bfloat16 [32, 128, 1024], P('grp', 'mlp'), may hold values from -5 to 5
- kv_pages: bfloat16 [32, 32, 128, 1024], P('grp', 'mlp'), may hold values from -5 to 5
- residual: bfloat16 [32, 128, 4096], P('grp'), may hold values from -3 to 3
- norm_gain: float32 [4096], replicated, may hold values from 0.5 to 1.5
- out_weight: bfloat16 [4096, 4096], P('mlp', 'grp'), may hold values from -0.09375 to 0.09375
- gate_weight: bfloat16 [4096, 6144], P('grp', 'mlp'), may hold values from -0.09375 to 0.09375
- up_weight: bfloat16 [4096, 6144], P('grp', 'mlp'), may hold values from -0.09375 to 0.09375
- down_weight: bfloat16 [6144, 4096], P('mlp', 'grp'), may hold values from -0.078125 to 0.078125
- page_table: int32 [32, 16, 12], P('grp'), may hold values from -1 to 31, as said below
- shared_pages: int32 [32, 4], P('grp'), may hold values from 0 to 31, as said below
- cache_lens: int32 [32, 16], P('grp'), may hold values from 513 to 2048, as said below
- prefill_offsets: int32 [32], P('grp'), may hold values from 1 to 512
Outputs:
- layer_out: bfloat16 [32, 128, 4096], P('grp', 'mlp')
Inputs may be any that keep to these rules, and one draw needn't show every extreme that they name: `page_table`: row d lists the pool pages that hold decode d's tokens after the shared prompt, in order, and -1 after its last page; no page appears twice in a group, and none is also a shared page. `shared_pages`: the pool pages of the group's shared prompt in order; they are the first 4 pages of every request of the group. `cache_lens`: decode d's cached tokens fill exactly its listed pages after the 4 shared pages; in every group one decode has the most.
All inputs are finite; a program needn't handle non-finite values.
Results may differ from a plain program's by a relative error of at most 0.029.
Values may be sent and summed in bfloat16 or wider, within the bound.
No kernel may reach another device: no remote copies, remote signals or barrier semaphores. Data moves between devices by JAX's collectives and lax.ppermute only.
A program may use at most 128 MiB of HBM per device.

v0:
```python
import jax
import jax.numpy as jnp
from jax import lax
from jax.sharding import PartitionSpec as P

HEADS = 32
KV_HEADS = 4
HEAD = 128
PAGE = 128
SHARED_PAGES = 4
PRIVATE_PAGES = 12
DECODES = 16
PREFILL = 112
ROWS = 128
NEG_FILL = -1e30
EPSILON = 1e-05


def merged(shard, axis, combine):
    everything = jax.tree.map(lambda part: lax.all_gather(part, axis), shard)
    leading = jax.tree.map(lambda part: part[0], everything)

    def step(k, so_far):
        return combine(so_far, jax.tree.map(lambda part: part[k], everything))

    return lax.fori_loop(1, lax.axis_size(axis), step, leading)


def page_layout(page_ids, table_group, shared_group):
    shared_match = shared_group[None, :] == page_ids[:, None]
    is_shared = jnp.any(shared_match, axis=1)
    shared_slot = jnp.sum(
        jnp.where(shared_match, jnp.arange(SHARED_PAGES, dtype=jnp.int32)[None, :], 0),
        axis=1,
        dtype=jnp.int32,
    )
    own_match = table_group[None, :, :] == page_ids[:, None, None]
    owner_id = (
        jnp.sum(
            jnp.where(own_match, jnp.arange(DECODES, dtype=jnp.int32)[None, :, None] + 1, 0),
            axis=(1, 2),
            dtype=jnp.int32,
        )
        - 1
    )
    own_slot = jnp.sum(
        jnp.where(own_match, jnp.arange(PRIVATE_PAGES, dtype=jnp.int32)[None, None, :], 0),
        axis=(1, 2),
        dtype=jnp.int32,
    )
    page_base = jnp.where(is_shared, shared_slot * PAGE, (SHARED_PAGES + own_slot) * PAGE)
    key_pos = (page_base[:, None] + jnp.arange(PAGE, dtype=jnp.int32)[None, :]).reshape(-1)
    key_shared = jnp.repeat(is_shared, PAGE)
    key_owner = jnp.repeat(jnp.where(is_shared, -1, owner_id), PAGE)
    return (key_pos, key_shared, key_owner)


def row_layout(lens_group, offset_value):
    row_ids = jnp.arange(ROWS, dtype=jnp.int32)
    is_prefill = row_ids < PREFILL
    decode_id = jnp.where(is_prefill, -2, row_ids - PREFILL)
    picked = decode_id[:, None] == jnp.arange(DECODES, dtype=jnp.int32)[None, :]
    decode_limit = jnp.sum(jnp.where(picked, lens_group[None, :], 0), axis=1, dtype=jnp.int32)
    limit = jnp.where(is_prefill, offset_value, decode_limit)
    return (row_ids, is_prefill, decode_id, limit)


def cache_visible(key_pos, key_shared, key_owner, decode_id, limit):
    belongs = key_shared[None, :] | (key_owner[None, :] == decode_id[:, None])
    return belongs & (key_pos[None, :] < limit[:, None])


def fresh_visible(key_rows, row_ids, is_prefill):
    before = (key_rows[None, :] < PREFILL) & (key_rows[None, :] <= row_ids[:, None])
    return jnp.where(is_prefill[:, None], before, key_rows[None, :] == row_ids[:, None])


def rms_norm(values, norm_gain):
    return (
        values * lax.rsqrt(jnp.mean(values * values, axis=1, keepdims=True) + EPSILON) * norm_gain
    ).astype(jnp.bfloat16)


def combine_parts(earlier_part, later_part):
    peak_one, total_one, mixed_one = earlier_part
    peak_two, total_two, mixed_two = later_part
    row_peak = jnp.maximum(peak_one, peak_two)
    factor_one = jnp.exp(peak_one - row_peak)
    factor_two = jnp.exp(peak_two - row_peak)
    row_total = total_one * factor_one + total_two * factor_two
    row_number, head_number = row_peak.shape
    weighted = (
        mixed_one.reshape(row_number, head_number, -1) * factor_one[:, :, None]
        + mixed_two.reshape(row_number, head_number, -1) * factor_two[:, :, None]
    )
    return (row_peak, row_total, weighted.reshape(row_number, -1))


def local(
    queries,
    fresh_kv,
    kv_pages,
    residual,
    norm_gain,
    out_weight,
    gate_weight,
    up_weight,
    down_weight,
    page_table,
    shared_pages,
    cache_lens,
    prefill_offsets,
):
    out_rows, gate_cols, up_cols, down_rows = (
        lax.all_gather(out_weight, "grp", axis=1, tiled=True),
        lax.all_gather(gate_weight, "grp", axis=0, tiled=True),
        lax.all_gather(up_weight, "grp", axis=0, tiled=True),
        lax.all_gather(down_weight, "grp", axis=1, tiled=True),
    )
    mlp_index = lax.axis_index("mlp")
    pool_pages = kv_pages.shape[1]
    own_count = fresh_kv.shape[1]
    page_ids = mlp_index * pool_pages + jnp.arange(pool_pages, dtype=jnp.int32)
    key_rows = mlp_index * own_count + jnp.arange(own_count, dtype=jnp.int32)
    key_pos, key_shared, key_owner = page_layout(page_ids, page_table[0], shared_pages[0])
    row_ids, is_prefill, decode_id, limit = row_layout(cache_lens[0], prefill_offsets[0])
    cache_seen = cache_visible(key_pos, key_shared, key_owner, decode_id, limit)
    fresh_seen = fresh_visible(key_rows, row_ids, is_prefill)
    cached = kv_pages[0].reshape(pool_pages * PAGE, 2, KV_HEADS, HEAD)
    fresh = fresh_kv[0].reshape(own_count, 2, KV_HEADS, HEAD)
    grouped = HEADS // KV_HEADS
    query_heads = queries[0].reshape(ROWS, KV_HEADS, grouped, HEAD)
    score_scale = HEAD ** (-0.5)
    peak_list = []
    total_list = []
    mixed_list = []
    for head_index in range(KV_HEADS):
        query_block = query_heads[:, head_index]
        cache_scores = (
            jnp.einsum(
                "rgh,kh->rgk",
                query_block,
                cached[:, 0, head_index],
                preferred_element_type=jnp.float32,
            )
            * score_scale
        )
        fresh_scores = (
            jnp.einsum(
                "rgh,kh->rgk",
                query_block,
                fresh[:, 0, head_index],
                preferred_element_type=jnp.float32,
            )
            * score_scale
        )
        cache_scores = jnp.where(cache_seen[:, None, :], cache_scores, NEG_FILL)
        fresh_scores = jnp.where(fresh_seen[:, None, :], fresh_scores, NEG_FILL)
        row_peak = jnp.maximum(jnp.max(cache_scores, axis=2), jnp.max(fresh_scores, axis=2))
        cache_exps = jnp.where(
            cache_seen[:, None, :], jnp.exp(cache_scores - row_peak[:, :, None]), 0.0
        )
        fresh_exps = jnp.where(
            fresh_seen[:, None, :], jnp.exp(fresh_scores - row_peak[:, :, None]), 0.0
        )
        row_total = jnp.sum(cache_exps, axis=2) + jnp.sum(fresh_exps, axis=2)
        weighted = jnp.einsum(
            "rgk,kh->rgh",
            cache_exps.astype(jnp.bfloat16),
            cached[:, 1, head_index],
            preferred_element_type=jnp.float32,
        )
        weighted = weighted + jnp.einsum(
            "rgk,kh->rgh",
            fresh_exps.astype(jnp.bfloat16),
            fresh[:, 1, head_index],
            preferred_element_type=jnp.float32,
        )
        peak_list.append(row_peak)
        total_list.append(row_total)
        mixed_list.append(weighted)
    row_peak = jnp.stack(peak_list, axis=1).reshape(ROWS, HEADS)
    row_total = jnp.stack(total_list, axis=1).reshape(ROWS, HEADS)
    weighted = jnp.stack(mixed_list, axis=1).reshape(ROWS, HEADS * HEAD)
    row_peak, row_total, weighted = merged((row_peak, row_total, weighted), "mlp", combine_parts)
    attended = (
        (weighted.reshape(ROWS, HEADS, HEAD) / row_total[:, :, None])
        .reshape(ROWS, HEADS * HEAD)
        .astype(jnp.bfloat16)
    )
    feature_count = out_rows.shape[0]
    own_features = lax.dynamic_slice_in_dim(attended, mlp_index * feature_count, feature_count, 1)
    row_begin = mlp_index * own_count
    projected = lax.psum(
        jnp.dot(own_features, out_rows, preferred_element_type=jnp.float32).astype(jnp.bfloat16),
        "mlp",
    ).astype(jnp.float32)
    updated = residual[0].astype(jnp.float32) + projected
    normed = rms_norm(updated, norm_gain)
    carried_rows = lax.dynamic_slice_in_dim(updated, row_begin, own_count, 0)
    gate_act = jnp.dot(normed, gate_cols, preferred_element_type=jnp.float32)
    up_act = jnp.dot(normed, up_cols, preferred_element_type=jnp.float32)
    hidden = (jax.nn.silu(gate_act) * up_act).astype(jnp.bfloat16)
    returned = lax.psum_scatter(
        jnp.dot(hidden, down_rows, preferred_element_type=jnp.float32).astype(jnp.bfloat16),
        "mlp",
        scatter_dimension=0,
        tiled=True,
    ).astype(jnp.float32)
    return (carried_rows + returned).astype(jnp.bfloat16)[None]


def solution(mesh):
    placed = (
        P("grp", None, None),
        P("grp", "mlp", None),
        P("grp", "mlp", None, None),
        P("grp", None, None),
        P(),
        P("mlp", "grp"),
        P("grp", "mlp"),
        P("grp", "mlp"),
        P("mlp", "grp"),
        P("grp", None, None),
        P("grp", None),
        P("grp", None),
        P("grp"),
    )
    return jax.shard_map(
        local, mesh=mesh, in_specs=placed, out_specs=P("grp", "mlp", None), check_vma=False
    )
```

profile of v0, /device:TPU:2, one launch (start us, length us, event | category | flops | bytes accessed | tf_op | source)
XLA Modules:
  0.0 786.7 jit_solution(5587190281900795073)
XLA Ops:
  21.2 2.0 fusion.102
  24.1 2.9 fusion.100
  37.2 2.4 fusion.17
  39.7 24.5 %all_gather.22 = f32[16,128,32]{1,2,0:T(8,128)S(1)} all-gather(f32[1,128,32]{1,2,0:T(8,128)S(1)} %maximum_bitcast_fusion.1), channel_id=1, replica_groups=mesh['grp'=32,'mlp'=16] {'mlp'}, dimensions={0}, use_global_device_ids=true | all-gather | bytes 278528 | tf_op jit(solution)/shard_map/all_gather | solution.py:20
  64.3 16.6 %all_gather.21 = f32[16,128,32]{1,2,0:T(8,128)S(1)} all-gather(f32[1,128,32]{1,2,0:T(8,128)S(1)} %maximum_bitcast_fusion), channel_id=1, replica_groups=mesh['grp'=32,'mlp'=16] {'mlp'}, dimensions={0}, use_global_device_ids=true | all-gather | bytes 278528 | tf_op jit(solution)/shard_map/all_gather | solution.py:20
  81.0 139.0 %all-gather.6.cloned.1.call-done = f32[16,128,4096]{2,1,0:T(8,128)} async-done(((f32[1,128,4096]{2,1,0:T(8,128)}), f32[16,128,4096]{2,1,0:T(8,128)}) %all-gather.6.cloned.1.call-update) | async-done | bytes 33554448 | tf_op jit(solution)/shard_map/all_gather | solution.py:20
  221.8 108.8 %while.19 = (s32[]{:T(128)}, f32[128,32]{1,0:T(8,128)S(1)}, f32[128,32]{1,0:T(8,128)S(1)}, f32[128,4096]{1,0:T(8,128)S(1)}, f32[16,128,32]{1,2,0:T(8,128)S(1)}, ...) while((s32[]{:T(128)}, f32[128,32]{1,0:T(8,128)S(1)}, ...), condition=%wide.region_22.23_spmd, body=%wide.region_21.22_spmd.sunk | while | flops 1597445 | bytes 14975127 | solution.py:26
  223.3 5.7 fusion.115
  230.6 5.7 fusion.115
  237.8 5.7 fusion.115
  245.1 5.7 fusion.115
  252.3 5.7 fusion.115
  259.6 5.7 fusion.115
  266.8 5.7 fusion.115
  274.1 5.7 fusion.115
  281.3 5.7 fusion.115
  288.6 5.7 fusion.115
  295.9 5.7 fusion.115
  303.1 5.7 fusion.115
  310.4 5.7 fusion.115
  317.6 5.7 fusion.115
  324.9 5.7 fusion.115
  331.2 3.0 copy.115
  334.2 3.2 convolution_convert_fusion.1
  339.2 114.0 %all-reduce.2.cloned.1.call-done = bf16[128,4096]{1,0:T(8,128)(2,1)} async-done(((bf16[128,4096]{1,0:T(8,128)(2,1)}), bf16[128,4096]{1,0:T(8,128)(2,1)}) %all-reduce.2.cloned.1.call-update) | async-done | bytes 1048592 | tf_op jit(solution)/shard_map/psum | solution.py:194
  453.3 3.0 convert_add_fusion
  456.2 84.0 %all-gather.10.cloned.1.call-done = bf16[4096,384]{1,0:T(8,128)(2,1)} async-done(((bf16[128,384]{1,0:T(8,128)(2,1)}), bf16[4096,384]{1,0:T(8,128)(2,1)}) %all-gather.10.cloned.1.call-update) | async-done | bytes 3145744 | tf_op jit(solution)/shard_map/all_gather | solution.py:116
  540.3 2.6 fusion.97
  542.9 83.0 %all-gather.12.cloned.1.call-done = bf16[4096,384]{1,0:T(8,128)(2,1)} async-done(((bf16[128,384]{1,0:T(8,128)(2,1)}), bf16[4096,384]{1,0:T(8,128)(2,1)}) %all-gather.12.cloned.1.call-update) | async-done | bytes 3145744 | tf_op jit(solution)/shard_map/all_gather | solution.py:117
  625.9 86.5 %all-gather.14.cloned.1.call-done = bf16[384,4096]{1,0:T(8,128)(2,1)} async-done(((bf16[384,128]{1,0:T(8,128)(2,1)}), bf16[384,4096]{1,0:T(8,128)(2,1)}) %all-gather.14.cloned.1.call-update) | async-done | bytes 3145744 | tf_op jit(solution)/shard_map/all_gather | solution.py:118
  712.5 5.3 convolution_convert_fusion
  717.8 60.5 %reduce-scatter.2.cloned.1.call-done = bf16[8,4096]{1,0:T(8,128)(2,1)} async-done(((bf16[128,4096]{1,0:T(8,128)(2,1)}), bf16[8,4096]{1,0:T(8,128)(2,1)}) %reduce-scatter.2.cloned.1.call-update) | async-done | bytes 65552 | tf_op jit(solution)/shard_map/reduce_scatter | solution.py:204
  (206 shorter events, 52.8 us)
Async XLA Ops:
  6.5 3.5 copy-start.16
  6.5 6.6 copy-start.15
  6.5 7.4 copy-start.8
  6.5 213.5 %all-gather.6.cloned.1.call-start = ((), (), s32[]{:S(2)}) async-start(), calls=%async_computation.1 | async-start | bytes 35651584 | tf_op jit(solution)/shard_map/all_gather | solution.py:20
  10.0 7.5 copy-start.7
  11.7 4.6 copy-start.20
  19.4 9.8 %copy-start.2 = (f32[128,8,256]{2,0,1:T(8,128)}, f32[128,8,256]{2,0,1:T(8,128)S(1)}, u32[]{:S(2)}) copy-start(f32[128,8,256]{2,0,1:T(8,128)S(1)} %get-tuple-element.256) | copy-start | bytes 3145732
  23.2 7.6 copy-start.4
  24.1 5.2 copy-start.10
  27.1 2.1 copy-start.19
  27.8 1.9 copy-start.11
  28.2 2.5 copy-start.18
  28.2 2.6 copy-start.9
  29.3 1.9 copy-start.12
  29.7 2.5 copy-start.17
  29.7 2.5 copy-start.6
  30.8 1.8 copy-start.13
  35.6 1.2 copy-start.3
  35.6 1.5 copy-start.5
  35.7 298.6 %all-gather.8.cloned.1.call-start = ((), (), s32[]{:S(2)}) async-start(), calls=%async_computation.2 | async-start | bytes 2162688 | tf_op jit(solution)/shard_map/all_gather | solution.py:115
  36.4 416.8 %all-reduce.2.cloned.1.call-start = ((), (), s32[]{:S(2)}) async-start(), calls=%async_computation.3 | async-start | bytes 2097152 | tf_op jit(solution)/shard_map/psum | solution.py:194
  334.2 119.0 %copy-start = (bf16[1,128,4096]{2,1,0:T(8,128)(2,1)S(1)}, bf16[1,128,4096]{2,1,0:T(8,128)(2,1)}, u32[]{:S(2)}) copy-start(bf16[1,128,4096]{2,1,0:T(8,128)(2,1)} %param.18) | copy-start | bytes 3145732
  337.4 202.8 %all-gather.10.cloned.1.call-start = ((), (), s32[]{:S(2)}) async-start(), calls=%async_computation.4 | async-start | bytes 3244032 | tf_op jit(solution)/shard_map/all_gather | solution.py:116
  338.0 287.9 %all-gather.12.cloned.1.call-start = ((), (), s32[]{:S(2)}) async-start(), calls=%async_computation.5 | async-start | bytes 3244032 | tf_op jit(solution)/shard_map/all_gather | solution.py:117
  338.6 373.9 %all-gather.14.cloned.1.call-start = ((), (), s32[]{:S(2)}) async-start(), calls=%async_computation.6 | async-start | bytes 3244032 | tf_op jit(solution)/shard_map/all_gather | solution.py:118
  339.2 201.1 %copy-start.14 = (f32[4096]{0:T(1024)S(1)}, f32[4096]{0:T(1024)}, u32[]{:S(2)}) copy-start(f32[4096]{0:T(1024)} %param.19) | copy-start | bytes 49156
  339.2 439.1 %reduce-scatter.2.cloned.1.call-start = ((), (), s32[]{:S(2)}) async-start(), calls=%async_computation.7 | async-start | bytes 1114112 | tf_op jit(solution)/shard_map/reduce_scatter | solution.py:204
  453.2 87.0 %copy-start.1 = (bf16[128,4096]{1,0:T(8,128)(2,1)S(1)}, bf16[128,4096]{1,0:T(8,128)(2,1)}, u32[]{:S(2)}) copy-start(bf16[128,4096]{1,0:T(8,128)(2,1)} %all-reduce.2.cloned.1.call-done) | copy-start | bytes 3145732
Sparse Core Ops, SparseCore 0:
  35.8 184.2 all-gather.5
  223.1 77.9 all-gather.7
  337.5 115.6 all-reduce.1
  456.7 83.4 all-gather.9
  543.8 82.1 all-gather.11
  629.3 83.1 all-gather.13
  717.9 60.2 reduce-scatter.1
where the time goes:
time: 788 us; the launch traced here: 787 us
  waiting for transfers between devices  569 us (72%)
  other arithmetic  97.4 us (12%)
  blocking collectives  41.1 us (5%)
  local copies, waits for them, and re-layouts  35.7 us (5%)
  matrix products  27.6 us (4%)
  between operations  14.6 us (2%)
    all_gather x1, waiting for transfers between devices, merged(): everything = jax.tree.map(lambda part: lax.all_gather(part, axis), shard)  139 us
    psum x1, waiting for transfers between devices, local(): lax.psum(jnp.dot(own_features, out_rows, preferred_element_type=jnp.float...  114 us
    all_gather x1, waiting for transfers between devices, local(): lax.all_gather(down_weight, 'grp', axis=1, tiled=True)  86.5 us
    add x15, other arithmetic, combine_parts(): mixed_one.reshape(row_number, head_number, -1) * factor_one[:, :, None]  86.1 us
    all_gather x1, waiting for transfers between devices, local(): lax.all_gather(gate_weight, 'grp', axis=0, tiled=True)  84 us
    all_gather x1, waiting for transfers between devices, local(): lax.all_gather(up_weight, 'grp', axis=0, tiled=True)  83 us
    reduce_scatter x1, waiting for transfers between devices, local(): lax.psum_scatter(jnp.dot(hidden, down_rows, preferred_element_type=jnp.fl...  60.5 us
    all_gather x2, blocking collectives, merged(): everything = jax.tree.map(lambda part: lax.all_gather(part, axis), shard)  41.1 us
  transfers between devices with their start and end apart: 7, of which 6 were waited for; matrix products, arithmetic and copies ran while one was open for 15% of the time, Pallas kernels for 0%

commit v1 on v0

--- a/solution.py
+++ b/solution.py
@@ -1,7 +1,9 @@
+import functools
 import jax
 import jax.numpy as jnp
 from jax import lax
 from jax.sharding import PartitionSpec as P
+from jax.lax import all_to_all, axis_size
 
 HEADS = 32
 KV_HEADS = 4
@@ -14,6 +16,22 @@
 ROWS = 128
 NEG_FILL = -1e30
 EPSILON = 1e-05
+
+
+def _order_flows(tile_in, out_dim):
+    arr_next = jnp.concatenate(
+        all_to_all(
+            jnp.stack([tile_in for _ in range(axis_size("grp"))], axis=0),
+            axis_name="grp",
+            split_axis=0,
+            concat_axis=0,
+        ),
+        axis=out_dim,
+    )
+    return arr_next
+
+
+_point_series = functools.partial(_order_flows, out_dim=0)
 
 
 def merged(shard, axis, combine):
@@ -114,7 +132,7 @@
     out_rows, gate_cols, up_cols, down_rows = (
         lax.all_gather(out_weight, "grp", axis=1, tiled=True),
         lax.all_gather(gate_weight, "grp", axis=0, tiled=True),
-        lax.all_gather(up_weight, "grp", axis=0, tiled=True),
+        _point_series(up_weight),
         lax.all_gather(down_weight, "grp", axis=1, tiled=True),
     )
     mlp_index = lax.axis_index("mlp")

time: 788 us -> 703 us (0.89)
  the two profiles are of different devices: /device:TPU:2 before, /device:TPU:16 now
where the time goes in v1:
time: 703 us; the launch traced here: 702 us
  waiting for transfers between devices  472 us (67%)
  other arithmetic  97.6 us (14%)
  blocking collectives  41.1 us (6%)
  local copies, waits for them, and re-layouts  37.9 us (5%)
  matrix products  27.9 us (4%)
  between operations  14.6 us (2%)
  starting transfers between devices  10 us (1%)
    all_gather x1, waiting for transfers between devices, merged(): everything = jax.tree.map(lambda part: lax.all_gather(part, axis), shard)  139 us
    psum x1, waiting for transfers between devices, local(): lax.psum(jnp.dot(own_features, out_rows, preferred_element_type=jnp.float...  104 us
    add x15, other arithmetic, combine_parts(): mixed_one.reshape(row_number, head_number, -1) * factor_one[:, :, None]  86.1 us
    all_gather x1, waiting for transfers between devices, local(): lax.all_gather(gate_weight, 'grp', axis=0, tiled=True)  84.2 us
    all_gather x1, waiting for transfers between devices, local(): lax.all_gather(down_weight, 'grp', axis=1, tiled=True)  81.3 us
    reduce_scatter x1, waiting for transfers between devices, local(): lax.psum_scatter(jnp.dot(hidden, down_rows, preferred_element_type=jnp.fl...  62 us
    all_gather x2, blocking collectives, merged(): everything = jax.tree.map(lambda part: lax.all_gather(part, axis), shard)  41.1 us
  transfers between devices with their start and end apart: 7, of which 5 were waited for; matrix products, arithmetic and copies ran while one was open for 18% of the time, Pallas kernels for 0%

profile of v1, /device:TPU:16, one launch (start us, length us, event | category | flops | bytes accessed | tf_op | source)
XLA Modules:
  0.0 702.1 jit_solution(1852616128215169947)
XLA Ops:
  24.1 2.9 fusion.100
  37.2 2.4 fusion.17
  39.7 24.5 %all_gather.19 = f32[16,128,32]{1,2,0:T(8,128)S(1)} all-gather(f32[1,128,32]{1,2,0:T(8,128)S(1)} %maximum_bitcast_fusion.1), channel_id=1, replica_groups=mesh['grp'=32,'mlp'=16] {'mlp'}, dimensions={0}, use_global_device_ids=true | all-gather | bytes 278528 | tf_op jit(solution)/shard_map/all_gather | solution.py:38
  64.3 16.6 %all_gather.18 = f32[16,128,32]{1,2,0:T(8,128)S(1)} all-gather(f32[1,128,32]{1,2,0:T(8,128)S(1)} %maximum_bitcast_fusion), channel_id=1, replica_groups=mesh['grp'=32,'mlp'=16] {'mlp'}, dimensions={0}, use_global_device_ids=true | all-gather | bytes 278528 | tf_op jit(solution)/shard_map/all_gather | solution.py:38
  81.0 138.9 %all-gather.5.cloned.1.call-done = f32[16,128,4096]{2,1,0:T(8,128)} async-done(((f32[1,128,4096]{2,1,0:T(8,128)}), f32[16,128,4096]{2,1,0:T(8,128)}) %all-gather.5.cloned.1.call-update) | async-done | bytes 33554448 | tf_op jit(solution)/shard_map/all_gather | solution.py:38
  221.6 108.8 %while.19 = (s32[]{:T(128)}, f32[128,32]{1,0:T(8,128)S(1)}, f32[128,32]{1,0:T(8,128)S(1)}, f32[128,4096]{1,0:T(8,128)S(1)}, f32[16,128,32]{1,2,0:T(8,128)S(1)}, ...) while((s32[]{:T(128)}, f32[128,32]{1,0:T(8,128)S(1)}, ...), condition=%wide.region_22.23_spmd, body=%wide.region_21.22_spmd.sunk | while | flops 1597445 | bytes 14975127 | solution.py:44
  223.1 5.7 fusion.115
  230.4 5.7 fusion.115
  237.7 5.7 fusion.115
  244.9 5.7 fusion.115
  252.2 5.7 fusion.115
  259.4 5.7 fusion.115
  266.7 5.7 fusion.115
  273.9 5.7 fusion.115
  281.2 5.7 fusion.115
  288.4 5.7 fusion.115
  295.7 5.7 fusion.115
  303.0 5.7 fusion.115
  310.2 5.7 fusion.115
  317.5 5.7 fusion.115
  324.7 5.7 fusion.115
  331.1 3.0 copy.115
  334.1 3.1 convolution_convert_fusion.1
  337.8 2.2 stack.23
  340.0 9.8 %all-to-all-start = ((bf16[32,128,384]{2,1,0:T(8,128)(2,1)}), bf16[32,128,384]{2,1,0:T(8,128)(2,1)S(1)}, u32[]{:S(2)}, u32[]{:S(2)}) async-start(bf16[32,128,384]{2,1,0:T(8,128)(2,1)} %stack.23), calls=%async_computation | async-start | bytes 6291456 | tf_op jit(solution)/shard_map/all_to_all | solution.py:23
  350.5 104.2 %all-reduce.2.cloned.1.call-done = bf16[128,4096]{1,0:T(8,128)(2,1)} async-done(((bf16[128,4096]{1,0:T(8,128)(2,1)}), bf16[128,4096]{1,0:T(8,128)(2,1)}) %all-reduce.2.cloned.1.call-update) | async-done | bytes 1048592 | tf_op jit(solution)/shard_map/psum | solution.py:212
  454.6 3.2 convert_add_fusion
  457.8 84.2 %all-gather.9.cloned.1.call-done = bf16[4096,384]{1,0:T(8,128)(2,1)} async-done(((bf16[128,384]{1,0:T(8,128)(2,1)}), bf16[4096,384]{1,0:T(8,128)(2,1)}) %all-gather.9.cloned.1.call-update) | async-done | bytes 3145744 | tf_op jit(solution)/shard_map/all_gather | solution.py:134
  542.0 3.3 fusion.97
  545.3 81.3 %all-gather.11.cloned.1.call-done = bf16[384,4096]{1,0:T(8,128)(2,1)} async-done(((bf16[384,128]{1,0:T(8,128)(2,1)}), bf16[384,4096]{1,0:T(8,128)(2,1)}) %all-gather.11.cloned.1.call-update) | async-done | bytes 3145744 | tf_op jit(solution)/shard_map/all_gather | solution.py:136
  626.7 5.0 convolution_convert_fusion
  631.7 62.0 %reduce-scatter.2.cloned.1.call-done = bf16[8,4096]{1,0:T(8,128)(2,1)} async-done(((bf16[128,4096]{1,0:T(8,128)(2,1)}), bf16[8,4096]{1,0:T(8,128)(2,1)}) %reduce-scatter.2.cloned.1.call-update) | async-done | bytes 65552 | tf_op jit(solution)/shard_map/reduce_scatter | solution.py:222
  (204 shorter events, 54.2 us)
Async XLA Ops:
  6.5 3.5 copy-start.15
  6.5 6.6 copy-start.14
  6.5 7.4 %copy-start.6 = (bf16[1,2,128,1024]{3,2,1,0:T(8,128)(2,1)S(1)}, bf16[1,2,128,1024]{3,2,1,0:T(8,128)(2,1)}, u32[]{:S(2)}) copy-start(bf16[1,2,128,1024]{3,2,1,0:T(8,128)(2,1)} %param.17) | copy-start | bytes 1572868
  6.5 213.3 %all-gather.5.cloned.1.call-start = ((), (), s32[]{:S(2)}) async-start(), calls=%async_computation.2 | async-start | bytes 35651584 | tf_op jit(solution)/shard_map/all_gather | solution.py:38
  10.0 7.5 %copy-start.5 = (bf16[1,128,4096]{1,2,0:T(8,128)(2,1)}, bf16[1,128,4096]{1,2,0:T(8,128)(2,1)S(1)}, u32[]{:S(2)}) copy-start(bf16[1,128,4096]{1,2,0:T(8,128)(2,1)S(1)} %copy.59) | copy-start | bytes 3145732
  11.7 4.6 copy-start.19
  19.4 9.8 %copy-start = (f32[128,8,256]{2,0,1:T(8,128)}, f32[128,8,256]{2,0,1:T(8,128)S(1)}, u32[]{:S(2)}) copy-start(f32[128,8,256]{2,0,1:T(8,128)S(1)} %get-tuple-element.256) | copy-start | bytes 3145732
  23.2 7.6 %copy-start.2 = (f32[128,8,256]{2,0,1:T(8,128)}, f32[128,8,256]{2,0,1:T(8,128)S(1)}, u32[]{:S(2)}) copy-start(f32[128,8,256]{2,0,1:T(8,128)S(1)} %get-tuple-element.252) | copy-start | bytes 3145732
  24.1 5.2 copy-start.8
  27.1 2.1 copy-start.18
  27.8 1.9 copy-start.9
  28.2 2.5 copy-start.17
  28.2 2.6 copy-start.7
  29.3 1.9 copy-start.10
  29.7 2.5 copy-start.16
  29.7 2.5 copy-start.4
  30.8 1.8 copy-start.11
  35.6 1.2 copy-start.1
  35.7 1.5 copy-start.3
  35.7 298.4 %all-gather.7.cloned.1.call-start = ((), (), s32[]{:S(2)}) async-start(), calls=%async_computation.3 | async-start | bytes 2162688 | tf_op jit(solution)/shard_map/all_gather | solution.py:133
  36.4 418.2 %all-reduce.2.cloned.1.call-start = ((), (), s32[]{:S(2)}) async-start(), calls=%async_computation.4 | async-start | bytes 2097152 | tf_op jit(solution)/shard_map/psum | solution.py:212
  334.1 3.7 copy-start.12
  337.2 204.8 %all-gather.9.cloned.1.call-start = ((), (), s32[]{:S(2)}) async-start(), calls=%async_computation.5 | async-start | bytes 3244032 | tf_op jit(solution)/shard_map/all_gather | solution.py:134
  340.0 205.3 %all-to-all-start = ((bf16[32,128,384]{2,1,0:T(8,128)(2,1)}), bf16[32,128,384]{2,1,0:T(8,128)(2,1)S(1)}, u32[]{:S(2)}, u32[]{:S(2)}) async-start(bf16[32,128,384]{2,1,0:T(8,128)(2,1)} %stack.23), calls=%async_computation | async-start | bytes 6291456 | tf_op jit(solution)/shard_map/all_to_all | solution.py:23
  349.8 276.9 %all-gather.11.cloned.1.call-start = ((), (), s32[]{:S(2)}) async-start(), calls=%async_computation.6 | async-start | bytes 3244032 | tf_op jit(solution)/shard_map/all_gather | solution.py:136
  350.4 191.6 %copy-start.13 = (f32[4096]{0:T(1024)S(1)}, f32[4096]{0:T(1024)}, u32[]{:S(2)}) copy-start(f32[4096]{0:T(1024)} %param.19) | copy-start | bytes 49156
  350.4 343.2 %reduce-scatter.2.cloned.1.call-start = ((), (), s32[]{:S(2)}) async-start(), calls=%async_computation.7 | async-start | bytes 1114112 | tf_op jit(solution)/shard_map/reduce_scatter | solution.py:222
Sparse Core Ops, SparseCore 0:
  35.8 184.0 all-gather.4
  222.9 77.3 all-gather.6
  337.3 117.2 all-reduce.1
  458.1 83.8 all-gather.8
  545.4 81.2 all-gather.10
  631.8 61.7 reduce-scatter.1
